TPU v7x, 32 devices: a whole 2x2x4 slice. The times are simulated.
32 devices in a mesh: groups: 2 (over x), ep: 16 (over z, y, core).
Axes of the slice: x: 2, y: 2, z: 4, core: 2. Of those that a mesh axis runs over, the one named last changes fastest.
Arguments:
- tokens: bfloat16 [2048, 3584], P(('groups', 'ep')), parts along dimension 0, may hold values from -6 to 6
- w_gate_up: bfloat16 [16, 3584, 512], P('ep'), may hold values from -0.09375 to 0.09375
- w_down: bfloat16 [16, 256, 3584], P('ep'), may hold values from -0.1875 to 0.1875
- w_copy_gate_up: bfloat16 [16, 3584, 512], P('ep'), may hold values from -0.09375 to 0.09375
- w_copy_down: bfloat16 [16, 256, 3584], P('ep'), may hold values from -0.1875 to 0.1875
- routes: int32 [2048, 2], P(('groups', 'ep')), parts along dimension 0, may hold values from 0 to 7, all different within a row; in each aligned block of 64 rows (0 to 63, 64 to 127, ...) at most 20 rows name the same one
- gate_weights: float32 [2048, 2], P(('groups', 'ep')), parts along dimension 0, may hold values from 0.1 to 1
- counts: int32 [32], P(('groups', 'ep')), parts along dimension 0, may hold values from 1 to 64, 768 in all
Outputs:
- moe_output: bfloat16 [2048, 3584], P(('groups', 'ep')), parts along dimension 0
There are 2 independent parts, one for each index of `groups`. A program takes and returns all parts, laid end to end along the dimension named above; an argument that names none is the same for every part. Nothing has to cross between parts.
Inputs may be any that keep to these rules, and one draw needn't show every extreme that they name: `routes`: each row names 2 different instances. Instances i and 4 + i live on devices 4 * i to 4 * i + 4 - 1 (team i). Among the rows of one device no instance is named by more than 20 rows.
All inputs are finite; a program needn't handle non-finite values. No bound on the sum of `counts` on one device may be relied on, other than what follows from the above.
Results may differ from a plain program's by a relative error of at most 0.0058.
Values may be sent and summed in bfloat16 or wider, within the bound.
A program may use at most 128 MiB of HBM per device.

v0:
```python
import jax
import jax.numpy as jnp
from jax import lax
from jax.sharding import PartitionSpec as P


def expert_pass(slot_block, gate_up_proj, down_proj):
    leading = slot_block.shape[:-1]
    feature_width = slot_block.shape[-1]
    hidden_units = down_proj.shape[0]
    flat_rows = slot_block.reshape(-1, feature_width)
    projected = jnp.dot(flat_rows, gate_up_proj, preferred_element_type=jnp.float32)
    hidden = (jax.nn.silu(projected[:, :hidden_units]) * projected[:, hidden_units:]).astype(
        jnp.bfloat16
    )
    result = jnp.dot(hidden, down_proj, preferred_element_type=jnp.float32).astype(jnp.bfloat16)
    return result.reshape(leading + (feature_width,))


def local(tokens, w_gate_up, w_down, w_copy_gate_up, w_copy_down, routes, gate_weights, counts):
    devices = lax.axis_size("ep")
    tok_rows, feature_width = tokens.shape
    route_count = routes.shape[1]
    split_ways = 4
    teams = devices // split_ways
    capacity = 5 * tok_rows * route_count // (8 * teams)
    own_gate_up = w_gate_up[0]
    own_down = w_down[0]
    copy_gate_up = w_copy_gate_up[0]
    copy_down = w_copy_down[0]
    entries = tok_rows * route_count
    flat_routes = routes.reshape(-1)
    live_rows = jnp.arange(tok_rows, dtype=jnp.int32) < counts[0]
    token_of = jnp.arange(entries, dtype=jnp.int32) // route_count
    alive_entry = live_rows[token_of]
    onehot = (
        (flat_routes[:, None] == jnp.arange(2 * teams, dtype=jnp.int32)[None, :])
        & alive_entry[:, None]
    ).astype(jnp.int32)
    rank_before = jnp.sum((jnp.cumsum(onehot, axis=0) - onehot) * onehot, axis=1)
    target_team = flat_routes % teams
    copy_flag = flat_routes // teams
    total_slots = teams * 2 * capacity
    slot_index = jnp.where(
        alive_entry, (target_team * 2 + copy_flag) * capacity + rank_before, total_slots
    )
    packed_rows = (
        jnp.zeros((total_slots + 1, feature_width), jnp.bfloat16)
        .at[slot_index]
        .set(tokens[token_of])[:total_slots]
    )
    packed = packed_rows.reshape(teams, 1, 2, capacity, feature_width)
    outgoing = jnp.broadcast_to(packed, (teams, split_ways, 2, capacity, feature_width)).reshape(
        devices, 2, capacity, feature_width
    )
    slot_block = lax.all_to_all(outgoing, "ep", split_axis=0, concat_axis=0, tiled=True)
    first_out = expert_pass(slot_block[:, 0], own_gate_up, own_down)
    second = expert_pass(slot_block[:, 1], copy_gate_up, copy_down)
    stacked = jnp.stack([first_out, second], axis=1)
    returned = lax.all_to_all(stacked, "ep", split_axis=0, concat_axis=0, tiled=True)
    merged = returned.reshape(teams, split_ways, 2, capacity, feature_width)
    summed = merged[:, 0].astype(jnp.float32)
    for quarter in range(1, split_ways):
        summed = summed + merged[:, quarter].astype(jnp.float32)
    summed = summed.reshape(total_slots, feature_width)
    picked = summed[jnp.minimum(slot_index, total_slots - 1)]
    weight = jnp.where(alive_entry, gate_weights.reshape(-1), 0.0)
    moe_output = jnp.sum(
        (picked * weight[:, None]).reshape(tok_rows, route_count, feature_width), axis=1
    )
    return moe_output.astype(jnp.bfloat16)


def solution(mesh):
    return jax.shard_map(
        local,
        mesh=mesh,
        in_specs=(
            P(("groups", "ep"), None),
            P("ep", None, None),
            P("ep", None, None),
            P("ep", None, None),
            P("ep", None, None),
            P(("groups", "ep"), None),
            P(("groups", "ep"), None),
            P(("groups", "ep")),
        ),
        out_specs=P(("groups", "ep"), None),
        check_vma=False,
    )
```

profile of v0, /device:TPU:9, one launch (start us, length us, event | category | flops | bytes accessed | tf_op | source)
XLA Modules:
  0.0 321.7 jit_solution(15467354852821212045)
XLA Ops:
  0.0 0.9 copy.24
  0.9 0.1 eq.17
  1.1 0.1 reshape.246
  1.9 1.2 gather_fusion
  3.2 0.2 reduce_window_sum.11
  3.4 0.2 select_reduce_fusion
  3.6 5.2 %scatter_custom_fusion = bf16[161,3584]{1,0:T(8,128)(2,1)S(1)} fusion(s32[128]{0:T(128)S(1)} %fusion.20, bf16[64,3584]{1,0:T(8,128)(2,1)} %param.8, s32[1024]{0:T(1024)S(1)} %pad_clamp_fusion.1, bf16[]{:T(256)} %constant.51.clone.1), kind=kCustom, calls=%fused_computation.17 | custom fusion | bytes 1154560 | tf_op jit(solution)/shard_map/scatter | solution.py:50
  8.8 1.1 slice.50
  9.9 1.4 broadcast_in_dim.27
  11.3 1.9 copy.26
  13.2 5.8 %broadcast_in_dim.28 = bf16[4,4,2,20,3584]{4,2,3,1,0:T(2,128)(2,1)} broadcast(bf16[4,2,20,3584]{3,1,2,0:T(2,128)(2,1)} %copy.26), dimensions={0,2,3,4} | broadcast | bytes 5734400 | tf_op jit(solution)/shard_map/broadcast_in_dim | solution.py:53
  19.0 108.0 %all_to_all.10 = bf16[16,2,20,3584]{3,1,2,0:T(2,128)(2,1)} all-to-all(bf16[16,2,20,3584]{3,1,2,0:T(2,128)(2,1)} %bitcast.34), channel_id=1, replica_groups=mesh['groups'=2,'ep'=16] {'ep'}, dimensions={0} | all-to-all | bytes 9175040 | tf_op jit(solution)/shard_map/all_to_all | solution.py:56
  127.0 24.0 %slice_reduce_fusion.1 = (bf16[16,20,3584]{2,1,0:T(8,128)(2,1)}, bf16[16,20,3584]{2,1,0:T(8,128)(2,1)}) fusion(bf16[16,2,20,3584]{3,1,2,0:T(2,128)(2,1)} %all_to_all.10), kind=kLoop, calls=%fused_computation.8 | loop fusion | bytes 9175040 | tf_op jit(solution)/shard_map/slice | solution.py:57
  151.0 4.1 %reshape_squeeze.6 = bf16[320,3584]{1,0:T(8,128)(2,1)} reshape(bf16[16,20,3584]{2,1,0:T(8,128)(2,1)} %get-tuple-element.5) | data formatting | bytes 4587520 | tf_op jit(solution)/shard_map/reshape;squeeze | solution.py:11
  155.2 4.1 %fusion.2 = f32[320,512]{1,0:T(8,128)S(1)} fusion(bf16[320,3584]{1,0:T(8,128)(2,1)} %reshape_squeeze.6, bf16[1,3584,512]{2,1,0:T(8,128)(2,1)} %param.9), kind=kOutput, calls=%fused_computation.11 | convolution fusion | flops 1174405120 | bytes 6619136 | tf_op jit(solution)/shard_map/dot_general | solution.py:12
  159.2 2.2 convolution_convert_fusion.1
  161.4 4.1 %stack_reshape.6 = bf16[16,1,20,3584]{3,2,0,1:T(8,128)(2,1)} reshape(bf16[320,3584]{1,0:T(8,128)(2,1)} %convolution_convert_fusion.1) | data formatting | bytes 4587520 | tf_op jit(solution)/shard_map/stack;reshape | solution.py:59
  165.5 4.1 %reshape_squeeze.7 = bf16[320,3584]{1,0:T(8,128)(2,1)} reshape(bf16[16,20,3584]{2,1,0:T(8,128)(2,1)} %get-tuple-element.6) | data formatting | bytes 4587520 | tf_op jit(solution)/shard_map/reshape;squeeze | solution.py:11
  169.7 4.2 %fusion = f32[320,512]{1,0:T(8,128)S(1)} fusion(bf16[320,3584]{1,0:T(8,128)(2,1)} %reshape_squeeze.7, bf16[1,3584,512]{2,1,0:T(8,128)(2,1)} %param.11), kind=kOutput, calls=%fused_computation.9 | convolution fusion | flops 1174405120 | bytes 6619136 | tf_op jit(solution)/shard_map/dot_general | solution.py:12
  173.9 2.2 convolution_convert_fusion
  176.1 4.1 %stack_reshape.7 = bf16[16,1,20,3584]{3,2,0,1:T(8,128)(2,1)} reshape(bf16[320,3584]{1,0:T(8,128)(2,1)} %convolution_convert_fusion) | data formatting | bytes 4587520 | tf_op jit(solution)/shard_map/stack;reshape | solution.py:59
  180.2 5.7 %pad_maximum_fusion = bf16[16,2,20,3584]{3,2,0,1:T(8,128)(2,1)} fusion(bf16[16,1,20,3584]{3,2,0,1:T(8,128)(2,1)} %stack_reshape.7, bf16[16,1,20,3584]{3,2,0,1:T(8,128)(2,1)} %stack_reshape.6), kind=kLoop, calls=%fused_computation.4 | loop fusion | flops 2293760 | bytes 9175040 | tf_op jit(solution)/shard_map/stack | solution.py:59
  185.9 9.3 %copy.27 = bf16[16,2,20,3584]{3,1,2,0:T(2,128)(2,1)} copy(bf16[16,2,20,3584]{3,2,0,1:T(8,128)(2,1)} %pad_maximum_fusion) | data formatting | bytes 9175040 | tf_op jit(solution)/shard_map/stack | solution.py:59
  195.2 4.9 %all-to-all-start.1 = ((bf16[16,2,20,3584]{3,1,2,0:T(2,128)(2,1)}), bf16[16,2,20,3584]{3,1,2,0:T(2,128)(2,1)}, u32[]{:S(2)}, u32[]{:S(2)}) async-start(bf16[16,2,20,3584]{3,1,2,0:T(2,128)(2,1)} %copy.27), calls=%async_computation.1 | async-start | bytes 9175040 | tf_op jit(solution)/shard_map/all_to_all | solution.py:60
  200.1 0.1 gather.20
  200.4 98.4 %all-to-all-done.1 = bf16[16,2,20,3584]{3,1,2,0:T(2,128)(2,1)} async-done(((bf16[16,2,20,3584]{3,1,2,0:T(2,128)(2,1)}), bf16[16,2,20,3584]{3,1,2,0:T(2,128)(2,1)}, u32[]{:S(2)}, u32[]{:S(2)}) %all-to-all-start.1) | async-done | bytes 4587552 | tf_op jit(solution)/shard_map/all_to_all | solution.py:60
  298.8 4.8 %fusion.24 = (bf16[4,1,2,20,3584]{4,2,3,1,0:T(2,128)(2,1)S(1)}, bf16[4,1,2,20,3584]{4,2,3,1,0:T(2,128)(2,1)S(1)}, bf16[4,1,2,20,3584]{4,2,3,1,0:T(2,128)(2,1)S(1)}, bf16[4,1,2,20,3584]{4,2,3,1,0:T(2,128)(2,1)S(1)}) fusion(bf16[4,4,2,20,3584]{4,2,3,1,0:T(2,128)(2,1)} %bitcast.10), kind=kLoop, calls=%fused_computation.55 | loop fusion | bytes 9175040 | tf_op jit(solution)/shard_map/slice | solution.py:62
  303.6 2.1 convert_add_fusion
  305.7 2.9 add.137
  308.7 4.9 %gather_fusion.1 = f32[128,3584]{1,0:T(8,128)} fusion(f32[160,3584]{1,0:T(8,128)} %add.137, s32[1024]{0:T(1024)S(1)} %pad_clamp_fusion), kind=kCustom, calls=%fused_computation.2 | custom fusion | bytes 3670528 | tf_op jit(solution)/shard_map/gather | solution.py:66
  313.6 3.3 %gather.19 = f32[64,2,3584]{2,1,0:T(2,128)} reshape(f32[128,3584]{1,0:T(8,128)} %gather_fusion.1) | data formatting | bytes 3670016 | tf_op jit(solution)/shard_map/gather | solution.py:66
  316.9 4.8 %multiply_reduce_fusion = bf16[64,3584]{1,0:T(8,128)(2,1)} fusion(f32[64,2,3584]{2,1,0:T(2,128)} %gather.19, f32[64,2]{1,0:T(8,128)S(1)} %broadcast_select_fusion), kind=kLoop, calls=%fused_computation.16 | loop fusion | flops 688128 | bytes 2294272 | tf_op jit(solution)/shard_map/reduce_sum | solution.py:68
  (17 shorter events, 0.3 us)
Async XLA Ops:
  0.0 159.2 %copy-start = (bf16[1,256,3584]{2,1,0:T(8,128)(2,1)S(1)}, bf16[1,256,3584]{2,1,0:T(8,128)(2,1)}, u32[]{:S(2)}) copy-start(bf16[1,256,3584]{2,1,0:T(8,128)(2,1)} %param.10) | copy-start | bytes 5505028
  169.7 4.2 %copy-start.3 = (bf16[1,256,3584]{2,1,0:T(8,128)(2,1)S(1)}, bf16[1,256,3584]{2,1,0:T(8,128)(2,1)}, u32[]{:S(2)}) copy-start(bf16[1,256,3584]{2,1,0:T(8,128)(2,1)} %param.12) | copy-start | bytes 5505028
  195.2 5.0 %copy-start.2 = (f32[64,2]{0,1:T(2,128)S(1)}, f32[64,2]{0,1:T(2,128)}, u32[]{:S(2)}) copy-start(f32[64,2]{0,1:T(2,128)} %param.14) | copy-start | bytes 1540
  195.2 103.6 %all-to-all-start.1 = ((bf16[16,2,20,3584]{3,1,2,0:T(2,128)(2,1)}), bf16[16,2,20,3584]{3,1,2,0:T(2,128)(2,1)}, u32[]{:S(2)}, u32[]{:S(2)}) async-start(bf16[16,2,20,3584]{3,1,2,0:T(2,128)(2,1)} %copy.27), calls=%async_computation.1 | async-start | bytes 9175040 | tf_op jit(solution)/shard_map/all_to_all | solution.py:60
  308.7 13.1 %copy-start.1 = (bf16[1,256,3584]{2,1,0:T(8,128)(2,1)S(1)}, bf16[1,256,3584]{2,1,0:T(8,128)(2,1)}, u32[]{:S(2)}) copy-start(bf16[1,256,3584]{2,1,0:T(8,128)(2,1)} %param.10) | copy-start | bytes 5505028
where the time goes:
time: 325 us; the launch traced here: 322 us
  blocking collectives  108 us (33%)
  waiting for transfers between devices  98.4 us (30%)
  local copies, waits for them, and re-layouts  83.8 us (26%)
  other arithmetic  13.2 us (4%)
  matrix products  12.6 us (4%)
  starting transfers between devices  4.86 us (1%)
    all_to_all x1, blocking collectives, local(): lax.all_to_all(outgoing, 'ep', split_axis=0, concat_axis=0, tiled=True)  108 us
    all_to_all x1, waiting for transfers between devices, local(): lax.all_to_all(stacked, 'ep', split_axis=0, concat_axis=0, tiled=True)  98.4 us
    slice x1, local copies, waits for them, and re-layouts, local(): first_out = expert_pass(slot_block[:, 0], own_gate_up, own_down)  24 us
    another operation x3, local copies, waits for them, and re-layouts, local(): stacked = jnp.stack([first_out, second], axis=1)  17.5 us
    broadcast_in_dim x3, local copies, waits for them, and re-layouts, local(): jnp.broadcast_to(packed, (teams, split_ways, 2, capacity, feature_width))  9.05 us
    dot_general x2, matrix products, expert_pass(): jnp.dot(flat_rows, gate_up_proj, preferred_element_type=jnp.float32)  8.27 us
    another operation x2, local copies, waits for them, and re-layouts, expert_pass(): flat_rows = slot_block.reshape(-1, feature_width)  8.24 us
    gather x2, local copies, waits for them, and re-layouts, local(): picked = summed[jnp.minimum(slot_index, total_slots - 1)]  8.24 us
  transfers between devices with their start and end apart: 1, of which 1 were waited for; matrix products, arithmetic and copies ran while one was open for 0% of the time, Pallas kernels for 0%

commit v1 on v0

v1 whole, which is shorter than its diff:
```python
import functools

import jax
import jax.numpy as jnp
from jax import lax
from jax.experimental import pallas as pl
from jax.experimental.pallas import tpu as pltpu
from jax.sharding import PartitionSpec as P

MESH = pl.DeviceIdType.MESH
BF = jnp.bfloat16
F32 = jnp.float32


def dot(a, b):
    return jnp.dot(a, b, preferred_element_type=F32)


def dot_nt(a, b):
    return lax.dot_general(a, b, (((1,), (1,)), ((), ())), preferred_element_type=F32)


def kernel(
    T, CAP, R, LO, HI,
    tok_ref, wg_ref, wd_ref, cg_ref, cd_ref, rt_ref, gw_ref, cnt_ref,
    out_ref,
    wg, wd, stk, gm, xs, X, pw, ps, pr, own, ys, yr, ks, zs, ret, fin,
    lsem, wsem, xsend, xrecv, tsend, trecv, dsem,
):
    TOK = tok_ref.shape[0]
    D = tok_ref.shape[1]
    H = D // 2
    HS = wd.shape[2]
    ep = lax.axis_index("ep")
    z = ep // 4
    y = (ep // 2) % 2
    c = ep % 2
    e_core = ep + 1 - 2 * c
    e_y = ep + 2 - 4 * y

    def src_plane(g):
        return lax.rem(z + g, T)

    def dst_plane(g):
        return lax.rem(z + T - g, T)

    def remote(src, dst, ssem, rsem, dev):
        return pltpu.make_async_remote_copy(
            src_ref=src, dst_ref=dst, send_sem=ssem, recv_sem=rsem,
            device_id={"ep": dev}, device_id_type=MESH,
        )

    def half(i):
        return pl.ds(pl.multiple_of(i * H, 128), H)

    wcopies = []
    for a, (gr, dr) in enumerate(((wg_ref, wd_ref), (cg_ref, cd_ref))):
        for h in range(2):
            wcopies.append(pltpu.make_async_copy(
                gr.at[0, pl.ds(h * H, H), :], wg.at[a, h], wsem.at[2 * a + h]))
            wcopies.append(pltpu.make_async_copy(
                dr.at[0, :, pl.ds(h * H, H)], wd.at[a, h], wsem.at[4 + 2 * a + h]))
    rows = pl.ds(pl.multiple_of(c * TOK, 16), TOK)
    lcopy = pltpu.make_async_copy(tok_ref.at[:, half(c)], stk.at[rows, :], lsem.at[0])
    lcopy.start()

    barrier = pltpu.get_barrier_semaphore()
    for g in range(1, T):
        pl.semaphore_signal(barrier, inc=1, device_id={"ep": lax.rem(z + g, T) * 4 + lax.rem(ep, 4)},
                            device_id_type=MESH)
    pl.semaphore_signal(barrier, inc=1, device_id={"ep": e_core}, device_id_type=MESH)
    pl.semaphore_signal(barrier, inc=1, device_id={"ep": e_y}, device_id_type=MESH)

    lane = lax.broadcasted_iota(jnp.int32, (TOK, 128), 1)
    row = lax.broadcasted_iota(jnp.int32, (TOK, 128), 0)
    live = row < cnt_ref[0]
    r0 = jnp.broadcast_to(rt_ref[:, 0:1], (TOK, 128))
    r1 = jnp.broadcast_to(rt_ref[:, 1:2], (TOK, 128))
    g0 = jnp.broadcast_to(gw_ref[:, 0:1], (TOK, 128))
    g1 = jnp.broadcast_to(gw_ref[:, 1:2], (TOK, 128))
    member = (lane == r0) | (lane == r1)
    gate = jnp.where(lane == r0 + 64, g0, jnp.where(lane == r1 + 64, g1, 0.0))
    mine = jnp.where(live, jnp.where(member, 1.0, gate), 0.0)
    mrow = pl.ds(pl.multiple_of(c * TOK, 16), TOK)
    gm[mrow, :] = mine

    pl.semaphore_wait(barrier, T + 1)

    tcopy = remote(tok_ref.at[:, half(1 - c)], stk.at[rows, :], tsend.at[0], trecv.at[0], e_core)
    mcopy = remote(gm.at[mrow, :], gm.at[mrow, :], tsend.at[1], trecv.at[1], e_core)
    mcopy.start()
    tcopy.start()
    for w in wcopies:
        w.start()

    n2 = 2 * TOK
    p = lax.broadcasted_iota(jnp.int32, (T, R, 128), 1).reshape(T * R, 128)
    team = lax.broadcasted_iota(jnp.int32, (T, R, 128), 0).reshape(T * R, 128)
    ln = lax.broadcasted_iota(jnp.int32, (T * R, 128), 1)
    one = lambda m: jnp.where(m, 1, 0)
    q = one(p >= CAP) + one(p >= 2 * CAP) + one(p >= 3 * CAP)
    copy_i = one(p >= 2 * CAP)
    core_i = q - 2 * copy_i
    rank_i = p - q * CAP
    valid = p < 4 * CAP
    inst = copy_i * T + team
    sel = jnp.where((ln == inst) & valid, 1.0, 0.0).astype(BF)
    selg = jnp.where((ln == inst + 64) & valid, 1.0, 0.0).astype(BF)
    tcore = one(ln >= TOK)
    ta = lax.broadcasted_iota(jnp.int32, (n2, n2), 0)
    tb = lax.broadcasted_iota(jnp.int32, (n2, n2), 1)
    low = jnp.where((tb < ta) & ((tb >= TOK) == (ta >= TOK)), 1.0, 0.0).astype(BF)

    mcopy.wait_recv()
    gall = gm[...]
    ghi = gall.astype(BF)
    glo = (gall - ghi.astype(F32)).astype(BF)
    rank = dot(low, ghi)
    a_m = dot_nt(sel, ghi)
    a_r = dot_nt(sel, rank.astype(BF))
    pick = (a_m > 0.5) & (a_r == rank_i.astype(F32)) & (tcore == core_i)
    pick = jnp.where(pick, 1.0, 0.0)
    pw[0] = (pick * dot_nt(selg, ghi)).astype(BF)
    pw[1] = (pick * dot_nt(selg, glo)).astype(BF)
    pw[2] = pick.astype(BF)
    lcopy.wait()
    tcopy.wait_recv()

    def zsend(g):
        return remote(xs.at[dst_plane(g)], X.at[z, y, c], xsend.at[0, g], xrecv.at[0, g],
                      dst_plane(g) * 4 + lax.rem(ep, 4))

    def zrecv(g):
        return remote(xs.at[src_plane(g)], X.at[src_plane(g), y, c], xsend.at[0, g], xrecv.at[0, g],
                      src_plane(g) * 4 + lax.rem(ep, 4))

    def ysend(g):
        s = src_plane(g)
        return remote(X.at[s, y, c], X.at[s, y, c], xsend.at[1, g], xrecv.at[1, g], e_y)

    def csend_a(g):
        s = src_plane(g)
        return remote(X.at[s, y, c], X.at[s, y, c], xsend.at[2, g], xrecv.at[2, g], e_core)

    def csend_b(g):
        s = src_plane(g)
        return remote(X.at[s, 1 - y, c], X.at[s, 1 - y, c], xsend.at[3, g], xrecv.at[3, g], e_core)

    def psend(g):
        return remote(ps.at[g], pr.at[g], xsend.at[4, g], xrecv.at[4, g], e_core)

    def rsend(g):
        return remote(ys.at[g], yr.at[g], xsend.at[5, g], xrecv.at[5, g], e_y)

    def bsend(g):
        return remote(zs.at[g], ret.at[z], xsend.at[6, g], xrecv.at[6, g],
                      src_plane(g) * 4 + lax.rem(ep, 4))

    def pack(i, carry):
        g = lax.rem(i + 1, T)
        d = dst_plane(g)
        o = pl.ds(pl.multiple_of(d * R, 16), R)
        blk = dot(pw[2, o, :], stk[...]).astype(BF)

        @pl.when(i < T - 1)
        def _():
            xs[d] = blk
            zsend(g).start()

        @pl.when(i == T - 1)
        def _():
            X[z, y, c] = blk

        return carry

    lax.fori_loop(0, T, pack, 0)
    for w in wcopies:
        w.wait()

    n0, n1 = HI, R - LO
    m0 = lax.broadcasted_iota(jnp.int32, (2, n0, HS), 1).reshape(2 * n0, HS) < 2 * CAP
    m1 = lax.broadcasted_iota(jnp.int32, (2, n1, HS), 1).reshape(2 * n1, HS) >= 2 * CAP - LO

    def hidden_of(s, a):
        lo, n, m = ((0, n0, m0), (LO, n1, m1))[a]
        acc = None
        for h in range(2):
            x = X[s, :, h, lo:lo + n, :].reshape(2 * n, H)
            v = dot(x, wg[a, h])
            acc = v if acc is None else acc + v
        gt, up = acc[:, :HS], acc[:, HS:]
        hid = gt / (1.0 + jnp.exp(-gt)) * up
        return jnp.where(m, hid, 0.0).astype(BF)

    def down(h0, h1, hh, store):
        o0 = dot(h0, wd[0, hh]).reshape(2, n0, H)
        o1 = dot(h1, wd[1, hh]).reshape(2, n1, H)
        if LO > 0:
            store(0, LO, o0[:, :LO])
        if HI > LO:
            store(LO, HI, o0[:, LO:] + o1[:, :HI - LO])
        if R > HI:
            store(HI, R, o1[:, HI - LO:])

    def step(k, carry):
        @pl.when(k < T)
        def _():
            @pl.when(k > 0)
            def _():
                zrecv(k).wait_recv()
            ysend(k).start()
            csend_a(k).start()

        @pl.when((k >= 1) & (k < T + 1))
        def _():
            g = k - 1
            s = src_plane(g)
            remote(X.at[s, 1 - y, c], X.at[s, 1 - y, c], xsend.at[1, g], xrecv.at[1, g], e_y).wait_recv()
            csend_b(g).start()

        @pl.when((k >= 1) & (k < T + 1))
        def _():
            g = k - 1
            s = src_plane(g)
            remote(X.at[s, y, 1 - c], X.at[s, y, 1 - c], xsend.at[2, g], xrecv.at[2, g], e_core).wait_recv()
            remote(X.at[s, 1 - y, 1 - c], X.at[s, 1 - y, 1 - c], xsend.at[3, g], xrecv.at[3, g],
                   e_core).wait_recv()
            h0 = hidden_of(s, 0)
            h1 = hidden_of(s, 1)

            def put(lo, hi, v):
                ps[g, :, lo:hi, :] = v.astype(BF)

            def keep(lo, hi, v):
                own[lax.rem(g, 2), :, lo:hi, :] = v

            down(h0, h1, 1 - c, put)
            psend(g).start()
            down(h0, h1, c, keep)

        @pl.when((k >= 2) & (k < T + 2))
        def _():
            g = k - 2
            psend(g).wait_recv()
            b = lax.rem(g, 2)
            ys[g] = (own[b, 1 - y] + pr[g, 1 - y].astype(F32)).astype(BF)
            rsend(g).start()
            ks[b] = own[b, y] + pr[g, y].astype(F32)

        @pl.when(k >= 3)
        def _():
            g = k - 3
            b = lax.rem(g, 2)
            rsend(g).wait_recv()
            v = (ks[b] + yr[g].astype(F32)).astype(BF)

            @pl.when(g > 0)
            def _():
                zs[g] = v
                bsend(g).start()

            @pl.when(g == 0)
            def _():
                ret[z] = v

        return carry

    lax.fori_loop(0, T + 3, step, 0)

    def got(g, carry):
        d = dst_plane(g)
        remote(zs.at[g], ret.at[d], xsend.at[6, g], xrecv.at[6, g], d * 4 + lax.rem(ep, 4)).wait_recv()
        return carry

    lax.fori_loop(1, T, got, 0)

    back = ret[...].reshape(T * R, H)
    w1 = pw[0].astype(F32).T.astype(BF)
    w2 = pw[1].astype(F32).T.astype(BF)
    fin[...] = (dot(w1, back) + dot(w2, back)).astype(BF)
    orow = pl.ds(pl.multiple_of((1 - c) * TOK, 16), TOK)
    fcopy = remote(fin.at[orow, :], out_ref.at[:, half(c)], tsend.at[2], trecv.at[2], e_core)
    fcopy.start()
    fl = pltpu.make_async_copy(fin.at[mrow, :], out_ref.at[:, half(c)], lsem.at[1])
    fl.start()

    def drain(g, carry):
        @pl.when(g > 0)
        def _():
            zsend(g).wait_send()
            bsend(g).wait_send()
        ysend(g).wait_send()
        csend_a(g).wait_send()
        csend_b(g).wait_send()
        psend(g).wait_send()
        rsend(g).wait_send()
        return carry

    lax.fori_loop(0, T, drain, 0)
    tcopy.wait_send()
    mcopy.wait_send()
    fl.wait()
    fcopy.wait_send()
    remote(fin.at[orow, :], out_ref.at[:, half(1 - c)], tsend.at[2], trecv.at[2], e_core).wait_recv()


def solution(mesh):
    devices = mesh.shape["ep"]
    T = devices // 4

    def local(tokens, w_gate_up, w_down, w_copy_gate_up, w_copy_down, routes, gate_weights, counts):
        tok, d = tokens.shape
        hs = w_down.shape[1]
        cap = 5 * tok * routes.shape[1] // (8 * T)
        R = -(-4 * cap // 16) * 16
        lo = 2 * cap // 16 * 16
        hi = -(-2 * cap // 16) * 16
        h = d // 2
        vm = pl.BlockSpec(memory_space=pltpu.VMEM)
        anym = pl.BlockSpec(memory_space=pl.ANY)
        return pl.pallas_call(
            functools.partial(kernel, T, cap, R, lo, hi),
            out_shape=jax.ShapeDtypeStruct((tok, d), BF),
            in_specs=[vm, anym, anym, anym, anym, vm, vm, pl.BlockSpec(memory_space=pltpu.SMEM)],
            out_specs=vm,
            scratch_shapes=[
                pltpu.VMEM((2, 2, h, 2 * hs), BF),
                pltpu.VMEM((2, 2, hs, h), BF),
                pltpu.VMEM((2 * tok, h), BF),
                pltpu.VMEM((2 * tok, 128), F32),
                pltpu.VMEM((T, R, h), BF),
                pltpu.VMEM((T, 2, 2, R, h), BF),
                pltpu.VMEM((3, T * R, 128), BF),
                pltpu.VMEM((T, 2, R, h), BF),
                pltpu.VMEM((T, 2, R, h), BF),
                pltpu.VMEM((2, 2, R, h), F32),
                pltpu.VMEM((T, R, h), BF),
                pltpu.VMEM((T, R, h), BF),
                pltpu.VMEM((2, R, h), F32),
                pltpu.VMEM((T, R, h), BF),
                pltpu.VMEM((T, R, h), BF),
                pltpu.VMEM((2 * tok, h), BF),
                pltpu.SemaphoreType.DMA((2,)),
                pltpu.SemaphoreType.DMA((8,)),
                pltpu.SemaphoreType.DMA((7, T)),
                pltpu.SemaphoreType.DMA((7, T)),
                pltpu.SemaphoreType.DMA((3,)),
                pltpu.SemaphoreType.DMA((3,)),
                pltpu.SemaphoreType.DMA((1,)),
            ],
            compiler_params=pltpu.CompilerParams(
                collective_id=0, has_side_effects=True, vmem_limit_bytes=60 * 1024 * 1024
            ),
        )(tokens, w_gate_up, w_down, w_copy_gate_up, w_copy_down, routes, gate_weights, counts)

    return jax.shard_map(
        local,
        mesh=mesh,
        in_specs=(
            P(("groups", "ep"), None),
            P("ep", None, None),
            P("ep", None, None),
            P("ep", None, None),
            P("ep", None, None),
            P(("groups", "ep"), None),
            P(("groups", "ep"), None),
            P(("groups", "ep")),
        ),
        out_specs=P(("groups", "ep"), None),
        check_vma=False,
    )
```

time: 325 us -> 89.1 us (0.27)
  blocking collectives: 108 us -> 0 us
  waiting for transfers between devices: 98.4 us -> 0 us
  Pallas kernels: 0 us -> 83.7 us
  local copies, waits for them, and re-layouts: 83.8 us -> 4.57 us
  other arithmetic: 13.2 us -> 0 us
  matrix products: 12.6 us -> 0 us
  starting transfers between devices: 4.86 us -> 0 us
    all_to_all x1 -> x0, blocking collectives: 108 us -> none  [local(): lax.all_to_all(outgoing, 'ep', split_axis=0, concat_axis=0, tiled=True)]
    all_to_all x1 -> x0, waiting for transfers between devices: 98.4 us -> none  [local(): lax.all_to_all(stacked, 'ep', split_axis=0, concat_axis=0, tiled=True)]
    pallas_call x0 -> x1, Pallas kernels: none -> 83.7 us  [local(): pl.pallas_call(functools.partial(kernel, T, cap, R, lo, hi), out_shape=ja...]
    slice x3 -> x0, local copies, waits for them, and re-layouts: 29.9 us -> none  [the longest x1 24 us: local(): first_out = expert_pass(slot_block[:, 0], own_gate_up, own_down)]
    another operation x5 -> x0, local copies, waits for them, and re-layouts: 25.8 us -> none  [the longest x3 17.5 us: local(): stacked = jnp.stack([first_out, second], axis=1)]
    dot_general x4 -> x0, matrix products: 12.6 us -> none  [the longest x2 8.27 us: expert_pass(): jnp.dot(flat_rows, gate_up_proj, preferred_element_type=jnp.float32)]
    gather x4 -> x0, local copies, waits for them, and re-layouts: 9.62 us -> none  [the longest x2 8.24 us: local(): picked = summed[jnp.minimum(slot_index, total_slots - 1)]]
    broadcast_in_dim x3 -> x0, local copies, waits for them, and re-layouts: 9.05 us -> none  [local(): jnp.broadcast_to(packed, (teams, split_ways, 2, capacity, feature_width))]
  transfers between devices with their start and end apart: 1 -> 0, of which waited for: 1 -> 0; matrix products, arithmetic and copies ran while one was open for 0% -> 0% of each run, Pallas kernels for 0% -> 0%
where the time goes in v1:
time: 89.1 us; the launch traced here: 88.9 us
  Pallas kernels  83.7 us (94%)
  local copies, waits for them, and re-layouts  4.57 us (5%)
    pallas_call x1, Pallas kernels, local(): pl.pallas_call(functools.partial(kernel, T, cap, R, lo, hi), out_shape=ja...  83.7 us
    unnamed x3, local copies, waits for them, and re-layouts  4.57 us

profile of v1, /device:TPU:9, one launch (start us, length us, event | category | flops | bytes accessed | tf_op | source)
XLA Modules:
  0.0 88.9 jit_solution(5996302736040716458)
XLA Ops:
  0.7 1.4 %copy.9.rt_ref = s32[64,2]{1,0:T(8,128)} copy(s32[64,2]{0,1:T(2,128)} %param.13) | data formatting | bytes 1024 | tf_op args[5]
  2.0 1.4 %copy.10.gw_ref = f32[64,2]{1,0:T(8,128)} copy(f32[64,2]{0,1:T(2,128)} %param.14) | data formatting | bytes 1024 | tf_op args[6]
  3.4 83.7 %shard_map.82 = bf16[64,3584]{1,0:T(8,128)(2,1)} custom-call(bf16[64,3584]{1,0:T(8,128)(2,1)} %tok_ref.1, bf16[1,3584,512]{2,1,0:T(8,128)(2,1)} %wg_ref.1, bf16[1,256,3584]{2,1,0:T(8,128)(2,1)} %wd_ref.1, bf16[1,3584,512]{2,1,0:T(8,128)(2,1)} %cg_ref.1, bf16[1,256,3584]{2,1,0:T(8,128)(2,1)} %cd_ref.1, s32[64,2]{1,0:T(8,128)} %copy.9.rt_ref, ...), custom_call_target="tpu_custom_call" | custom-call | tf_op jit(solution)/shard_map/pallas_call | solution.py:321
  87.1 1.8 %copy.13 = bf16[64,3584]{1,0:T(8,128)(2,1)} copy(bf16[64,3584]{1,0:T(8,128)(2,1)} %shard_map.82) | data formatting | bytes 917504

commit v2 on v1

v2 whole, which is shorter than its diff:
```python
import functools

import jax
import jax.numpy as jnp
from jax import lax
from jax.experimental import pallas as pl
from jax.experimental.pallas import tpu as pltpu
from jax.sharding import PartitionSpec as P

MESH = pl.DeviceIdType.MESH
BF = jnp.bfloat16
F32 = jnp.float32


def dot(a, b):
    return jnp.dot(a, b, preferred_element_type=F32)


def kernel(
    T, CAP, R, LO, HI, NC,
    tok_ref, wg_ref, wd_ref, cg_ref, cd_ref, rt_ref, gw_ref, cnt_ref,
    out_ref,
    wg, wd, stk, gm, xs, X, pw, ps, pr, own, ys, yr, ks, zs, ret, fin,
    lsem, wsem, xsend, xrecv, tsend, trecv,
):
    TOK = tok_ref.shape[0]
    TR = T * R
    D = tok_ref.shape[1]
    H = D // 2
    HC = H // NC
    HS = wd.shape[3]
    ep = lax.axis_index("ep")
    z = ep // 4
    y = (ep // 2) % 2
    c = ep % 2
    e_core = ep + 1 - 2 * c
    e_y = ep + 2 - 4 * y

    def src_plane(g):
        return lax.rem(z + g, T)

    def dst_plane(g):
        return lax.rem(z + T - g, T)

    def remote(src, dst, ssem, rsem, dev):
        return pltpu.make_async_remote_copy(
            src_ref=src, dst_ref=dst, send_sem=ssem, recv_sem=rsem,
            device_id={"ep": dev}, device_id_type=MESH,
        )

    def half(i):
        return pl.ds(pl.multiple_of(i * H, 128), H)

    wcopies = []
    for a, (gr, dr) in enumerate(((wg_ref, wd_ref), (cg_ref, cd_ref))):
        wcopies.append(pltpu.make_async_copy(gr.at[0], wg.at[a], wsem.at[0, a]))
        for h in range(2):
            for j in range(NC):
                wcopies.append(pltpu.make_async_copy(
                    dr.at[0, :, pl.ds(h * H + j * HC, HC)], wd.at[a, h, j], wsem.at[1 + h, a * NC + j]))
    rows = pl.ds(pl.multiple_of(c * TOK, 16), TOK)
    lcopy = pltpu.make_async_copy(tok_ref.at[:, half(c)], stk.at[rows, :], lsem.at[0])
    lcopy.start()

    barrier = pltpu.get_barrier_semaphore()
    for g in range(1, T):
        pl.semaphore_signal(barrier, inc=1, device_id={"ep": lax.rem(z + g, T) * 4 + lax.rem(ep, 4)},
                            device_id_type=MESH)
    pl.semaphore_signal(barrier, inc=1, device_id={"ep": e_core}, device_id_type=MESH)
    pl.semaphore_signal(barrier, inc=1, device_id={"ep": e_y}, device_id_type=MESH)

    n2 = 2 * TOK
    lane = lax.broadcasted_iota(jnp.int32, (128, n2), 1)
    row = lax.broadcasted_iota(jnp.int32, (128, n2), 0)
    off = lane - c * TOK
    live = (off >= 0) & (off < cnt_ref[0])
    twice = lambda v: jnp.broadcast_to(jnp.concatenate([v, v], axis=1), (128, n2))
    r0, r1 = twice(rt_ref[0:1, :]), twice(rt_ref[1:2, :])
    g0, g1 = twice(gw_ref[0:1, :]), twice(gw_ref[1:2, :])
    member = (row == r0) | (row == r1)
    gate = jnp.where(row == r0 + 64, g0, jnp.where(row == r1 + 64, g1, 0.0))
    gm[c] = jnp.where(live, jnp.where(member, 1.0, gate), 0.0)
    mrow = pl.ds(pl.multiple_of(c * TOK, 16), TOK)

    pl.semaphore_wait(barrier, T + 1)

    tcopy = remote(tok_ref.at[:, half(1 - c)], stk.at[rows, :], tsend.at[0], trecv.at[0], e_core)
    mcopy = remote(gm.at[c], gm.at[c], tsend.at[1], trecv.at[1], e_core)
    mcopy.start()
    tcopy.start()
    for w in wcopies:
        w.start()

    p = lax.broadcasted_iota(jnp.int32, (T, R, 128), 1).reshape(T * R, 128)
    team = lax.broadcasted_iota(jnp.int32, (T, R, 128), 0).reshape(T * R, 128)
    ln = lax.broadcasted_iota(jnp.int32, (T * R, 128), 1)
    one = lambda m: jnp.where(m, 1, 0)
    q = one(p >= CAP) + one(p >= 2 * CAP) + one(p >= 3 * CAP)
    copy_i = one(p >= 2 * CAP)
    core_i = q - 2 * copy_i
    rank_i = p - q * CAP
    valid = p < 4 * CAP
    inst = copy_i * T + team
    sel = jnp.where((ln == inst) & valid, 1.0, 0.0).astype(BF)
    selg = jnp.where((ln == inst + 64) & valid, 1.0, 0.0).astype(BF)
    tcore = one(ln >= TOK)
    ta = lax.broadcasted_iota(jnp.int32, (n2, n2), 0)
    tb = lax.broadcasted_iota(jnp.int32, (n2, n2), 1)
    low = jnp.where((ta < tb) & ((tb >= TOK) == (ta >= TOK)), 1.0, 0.0).astype(BF)

    mcopy.wait_recv()
    gall = gm[0] + gm[1]
    ghi = gall.astype(BF)
    glo = (gall - ghi.astype(F32)).astype(BF)
    rank = dot(ghi, low)
    a_m = dot(sel, ghi)
    a_r = dot(sel, rank.astype(BF))
    pick = (a_m > 0.5) & (a_r == rank_i.astype(F32)) & (tcore == core_i)
    pick = jnp.where(pick, 1.0, 0.0)
    pw[0] = (pick * dot(selg, ghi)).astype(BF)
    pw[1] = (pick * dot(selg, glo)).astype(BF)
    pw[2] = pick.astype(BF)
    lcopy.wait()
    tcopy.wait_recv()

    def zsend(g, j):
        return remote(xs.at[dst_plane(g), j], X.at[z, y, c, j], xsend.at[0, g, j], xrecv.at[0, g, j],
                      dst_plane(g) * 4 + lax.rem(ep, 4))

    def zrecv(g, j):
        s = src_plane(g)
        return remote(xs.at[s, j], X.at[s, y, c, j], xsend.at[0, g, j], xrecv.at[0, g, j], s * 4 + lax.rem(ep, 4))

    def xcopy(n, s, yy, cc, g, j, dev):
        r = X.at[s, yy, cc, j]
        return remote(r, r, xsend.at[n, g, j], xrecv.at[n, g, j], dev)

    def ysend(g, j):
        return xcopy(1, src_plane(g), y, c, g, j, e_y)

    def csend_a(g, j):
        return xcopy(2, src_plane(g), y, c, g, j, e_core)

    def csend_b(g, j):
        return xcopy(3, src_plane(g), 1 - y, c, g, j, e_core)

    def psend(g, j):
        return remote(ps.at[g, j], pr.at[g, j], xsend.at[4, g, j], xrecv.at[4, g, j], e_core)

    def rsend(g, j):
        return remote(ys.at[g, j], yr.at[g, j], xsend.at[5, g, j], xrecv.at[5, g, j], e_y)

    def bsend(g, j):
        return remote(zs.at[g, j], ret.at[j, z], xsend.at[6, g, j], xrecv.at[6, g, j],
                      src_plane(g) * 4 + lax.rem(ep, 4))

    def pack(i, carry):
        g = lax.rem(i + 1, T)
        d = dst_plane(g)
        o = pl.ds(pl.multiple_of(d * R, 16), R)
        for j in range(NC):
            blk = dot(pw[2, o, :], stk[:, j * HC:(j + 1) * HC]).astype(BF)

            @pl.when(i < T - 1)
            def _():
                xs[d, j] = blk
                zsend(g, j).start()

            @pl.when(i == T - 1)
            def _():
                X[z, y, c, j] = blk
                ysend(0, j).start()
                csend_a(0, j).start()

        return carry

    lax.fori_loop(0, T, pack, 0)

    n0, n1 = HI, R - LO
    m0 = lax.broadcasted_iota(jnp.int32, (2, n0, HS), 1).reshape(2 * n0, HS) < 2 * CAP
    m1 = lax.broadcasted_iota(jnp.int32, (2, n1, HS), 1).reshape(2 * n1, HS) >= 2 * CAP - LO

    def hidden_of(s, a):
        lo, n, m = ((0, n0, m0), (LO, n1, m1))[a]
        acc = None
        for h in range(2):
            for j in range(NC):
                x = X[s, :, h, j, lo:lo + n, :].reshape(2 * n, HC)
                v = dot(x, wg[a, h * H + j * HC:h * H + (j + 1) * HC, :])
                acc = v if acc is None else acc + v
        gt, up = acc[:, :HS], acc[:, HS:]
        hid = gt / (1.0 + jnp.exp(-gt)) * up
        return jnp.where(m, hid, 0.0).astype(BF)

    def down(h0, h1, hh, j, store):
        o0 = dot(h0, wd[0, hh, j]).reshape(2, n0, HC)
        o1 = dot(h1, wd[1, hh, j]).reshape(2, n1, HC)
        if LO > 0:
            store(0, LO, o0[:, :LO])
        if HI > LO:
            store(LO, HI, o0[:, LO:] + o1[:, :HI - LO])
        if R > HI:
            store(HI, R, o1[:, HI - LO:])

    def step(k, carry):
        @pl.when((k > 0) & (k < T))
        def _():
            for j in range(NC):
                zrecv(k, j).wait_recv()
                ysend(k, j).start()
                csend_a(k, j).start()

        @pl.when((k >= 1) & (k < T + 1))
        def _():
            g = k - 1
            s = src_plane(g)
            for j in range(NC):
                xcopy(1, s, 1 - y, c, g, j, e_y).wait_recv()
                csend_b(g, j).start()

            @pl.when(k == 1)
            def _():
                for w in wcopies:
                    w.wait()

            for j in range(NC):
                xcopy(2, s, y, 1 - c, g, j, e_core).wait_recv()
                xcopy(3, s, 1 - y, 1 - c, g, j, e_core).wait_recv()
            h0 = hidden_of(s, 0)
            h1 = hidden_of(s, 1)
            for j in range(NC):
                def put(lo, hi, v, j=j):
                    ps[g, j, :, lo:hi, :] = v.astype(BF)

                down(h0, h1, 1 - c, j, put)
                psend(g, j).start()
            for j in range(NC):
                def keep(lo, hi, v, j=j):
                    own[j, :, lo:hi, :] = v

                down(h0, h1, c, j, keep)

        @pl.when(k >= 2)
        def _():
            g = k - 2
            for j in range(NC):
                rsend(g, j).wait_recv()
                v = (ks[j] + yr[g, j].astype(F32)).astype(BF)

                @pl.when(g > 0)
                def _():
                    zs[g, j] = v
                    bsend(g, j).start()

                @pl.when(g == 0)
                def _():
                    ret[j, z] = v

        @pl.when((k >= 1) & (k < T + 1))
        def _():
            g = k - 1
            for j in range(NC):
                psend(g, j).wait_recv()
                ys[g, j] = (own[j, 1 - y] + pr[g, j, 1 - y].astype(F32)).astype(BF)
                rsend(g, j).start()
                ks[j] = own[j, y] + pr[g, j, y].astype(F32)

        return carry

    lax.fori_loop(0, T + 2, step, 0)

    w1 = pw[0].astype(F32).T.astype(BF)
    w2 = pw[1].astype(F32).T.astype(BF)
    orow = pl.ds(pl.multiple_of((1 - c) * TOK, 16), TOK)
    fl = []
    fc = []
    for j in range(NC):
        def got(g, carry, j=j):
            d = dst_plane(g)
            remote(zs.at[g, j], ret.at[j, d], xsend.at[6, g, j], xrecv.at[6, g, j],
                   d * 4 + lax.rem(ep, 4)).wait_recv()
            return carry

        lax.fori_loop(1, T, got, 0)
        back = ret[j].reshape(TR, HC)
        fin[j] = (dot(w1, back) + dot(w2, back)).astype(BF)

        def cols(i, j=j):
            return pl.ds(pl.multiple_of(i * H + j * HC, 128), HC)

        fc.append(remote(fin.at[j, orow, :], out_ref.at[:, cols(c)], tsend.at[2 + j], trecv.at[2 + j], e_core))
        fc[-1].start()
        fl.append(pltpu.make_async_copy(fin.at[j, mrow, :], out_ref.at[:, cols(c)], lsem.at[1 + j]))
        fl[-1].start()

    def drain(g, carry):
        for j in range(NC):
            @pl.when(g > 0)
            def _():
                zsend(g, j).wait_send()
                bsend(g, j).wait_send()
            ysend(g, j).wait_send()
            csend_a(g, j).wait_send()
            csend_b(g, j).wait_send()
            psend(g, j).wait_send()
            rsend(g, j).wait_send()
        return carry

    lax.fori_loop(0, T, drain, 0)
    tcopy.wait_send()
    mcopy.wait_send()
    for j in range(NC):
        fl[j].wait()
        fc[j].wait_send()
        cc = pl.ds(pl.multiple_of((1 - c) * H + j * HC, 128), HC)
        remote(fin.at[j, orow, :], out_ref.at[:, cc], tsend.at[2 + j], trecv.at[2 + j], e_core).wait_recv()


NC = 2


def solution(mesh):
    devices = mesh.shape["ep"]
    T = devices // 4

    def local(tokens, w_gate_up, w_down, w_copy_gate_up, w_copy_down, routes, gate_weights, counts):
        tok, d = tokens.shape
        hs = w_down.shape[1]
        cap = 5 * tok * routes.shape[1] // (8 * T)
        R = -(-4 * cap // 16) * 16
        lo = 2 * cap // 16 * 16
        hi = -(-2 * cap // 16) * 16
        h = d // 2
        hc = h // NC
        vm = pl.BlockSpec(memory_space=pltpu.VMEM)
        anym = pl.BlockSpec(memory_space=pl.ANY)
        return pl.pallas_call(
            functools.partial(kernel, T, cap, R, lo, hi, NC),
            out_shape=jax.ShapeDtypeStruct((tok, d), BF),
            in_specs=[anym, anym, anym, anym, anym, vm, vm, pl.BlockSpec(memory_space=pltpu.SMEM)],
            out_specs=vm,
            scratch_shapes=[
                pltpu.VMEM((2, d, 2 * hs), BF),
                pltpu.VMEM((2, 2, NC, hs, hc), BF),
                pltpu.VMEM((2 * tok, h), BF),
                pltpu.VMEM((2, 128, 2 * tok), F32),
                pltpu.VMEM((T, NC, R, hc), BF),
                pltpu.VMEM((T, 2, 2, NC, R, hc), BF),
                pltpu.VMEM((3, T * R, 128), BF),
                pltpu.VMEM((T, NC, 2, R, hc), BF),
                pltpu.VMEM((T, NC, 2, R, hc), BF),
                pltpu.VMEM((NC, 2, R, hc), F32),
                pltpu.VMEM((T, NC, R, hc), BF),
                pltpu.VMEM((T, NC, R, hc), BF),
                pltpu.VMEM((NC, R, hc), F32),
                pltpu.VMEM((T, NC, R, hc), BF),
                pltpu.VMEM((NC, T, R, hc), BF),
                pltpu.VMEM((NC, 2 * tok, hc), BF),
                pltpu.SemaphoreType.DMA((1 + NC,)),
                pltpu.SemaphoreType.DMA((3, 2 * NC)),
                pltpu.SemaphoreType.DMA((7, T, NC)),
                pltpu.SemaphoreType.DMA((7, T, NC)),
                pltpu.SemaphoreType.DMA((2 + NC,)),
                pltpu.SemaphoreType.DMA((2 + NC,)),
            ],
            compiler_params=pltpu.CompilerParams(
                collective_id=0, has_side_effects=True, vmem_limit_bytes=60 * 1024 * 1024
            ),
        )(tokens, w_gate_up, w_down, w_copy_gate_up, w_copy_down, routes.T, gate_weights.T, counts)

    return jax.shard_map(
        local,
        mesh=mesh,
        in_specs=(
            P(("groups", "ep"), None),
            P("ep", None, None),
            P("ep", None, None),
            P("ep", None, None),
            P("ep", None, None),
            P(("groups", "ep"), None),
            P(("groups", "ep"), None),
            P(("groups", "ep")),
        ),
        out_specs=P(("groups", "ep"), None),
        check_vma=False,
    )
```

time: 89.1 us -> 76.7 us (0.86); the launches traced: 88.9 us -> 75.3 us
  Pallas kernels: 83.7 us -> 72.8 us
  local copies, waits for them, and re-layouts: 4.57 us -> 1.82 us
    pallas_call x1, Pallas kernels: 83.7 us -> 72.8 us  [local(): pl.pallas_call(functools.partial(kernel, T, cap, R, lo, hi, NC), out_shap...]
    unnamed x3 -> x1, local copies, waits for them, and re-layouts: 4.57 us -> 1.82 us
where the time goes in v2:
time: 76.7 us; the launch traced here: 75.3 us
  Pallas kernels  72.8 us (95%)
  local copies, waits for them, and re-layouts  1.82 us (2%)
    pallas_call x1, Pallas kernels, local(): pl.pallas_call(functools.partial(kernel, T, cap, R, lo, hi, NC), out_shap...  72.8 us
    unnamed x1, local copies, waits for them, and re-layouts  1.82 us

profile of v2, /device:TPU:9, one launch (start us, length us, event | category | flops | bytes accessed | tf_op | source)
XLA Modules:
  0.0 75.3 jit_solution(14671207254913787871)
XLA Ops:
  0.7 72.8 %shard_map.82 = bf16[64,3584]{1,0:T(8,128)(2,1)} custom-call(bf16[64,3584]{1,0:T(8,128)(2,1)} %tok_ref.1, bf16[1,3584,512]{2,1,0:T(8,128)(2,1)} %wg_ref.1, bf16[1,256,3584]{2,1,0:T(8,128)(2,1)} %wd_ref.1, bf16[1,3584,512]{2,1,0:T(8,128)(2,1)} %cg_ref.1, bf16[1,256,3584]{2,1,0:T(8,128)(2,1)} %cd_ref.1, s32[2,64]{1,0:T(2,128)} %bitcast.2, f32[2,64]{1,0:T(2,128)} %bitcast.3, ...), custom_call_target="tpu_custom_call" | custom-call | tf_op jit(solution)/shard_map/pallas_call | solution.py:337
  73.5 1.8 %copy.11 = bf16[64,3584]{1,0:T(8,128)(2,1)} copy(bf16[64,3584]{1,0:T(8,128)(2,1)} %shard_map.82) | data formatting | bytes 917504

commit v3 on v2

--- a/solution.py
+++ b/solution.py
@@ -20,7 +20,7 @@
     T, CAP, R, LO, HI, NC,
     tok_ref, wg_ref, wd_ref, cg_ref, cd_ref, rt_ref, gw_ref, cnt_ref,
     out_ref,
-    wg, wd, stk, gm, xs, X, pw, ps, pr, own, ys, yr, ks, zs, ret, fin,
+    wg, wd, stk, gm, xs, X, pw, ps, pr, own, ys, yr, ks, zs, ret, fin, wt,
     lsem, wsem, xsend, xrecv, tsend, trecv,
 ):
     TOK = tok_ref.shape[0]
@@ -88,8 +88,6 @@
     mcopy = remote(gm.at[c], gm.at[c], tsend.at[1], trecv.at[1], e_core)
     mcopy.start()
     tcopy.start()
-    for w in wcopies:
-        w.start()
 
     p = lax.broadcasted_iota(jnp.int32, (T, R, 128), 1).reshape(T * R, 128)
     team = lax.broadcasted_iota(jnp.int32, (T, R, 128), 0).reshape(T * R, 128)
@@ -122,6 +120,8 @@
     pw[2] = pick.astype(BF)
     lcopy.wait()
     tcopy.wait_recv()
+    for w in wcopies:
+        w.start()
 
     def zsend(g, j):
         return remote(xs.at[dst_plane(g), j], X.at[z, y, c, j], xsend.at[0, g, j], xrecv.at[0, g, j],
@@ -155,18 +155,21 @@
                       src_plane(g) * 4 + lax.rem(ep, 4))
 
     def pack(i, carry):
-        g = lax.rem(i + 1, T)
+        g = i
         d = dst_plane(g)
         o = pl.ds(pl.multiple_of(d * R, 16), R)
         for j in range(NC):
             blk = dot(pw[2, o, :], stk[:, j * HC:(j + 1) * HC]).astype(BF)
 
-            @pl.when(i < T - 1)
+            @pl.when(i > 0)
             def _():
                 xs[d, j] = blk
-                zsend(g, j).start()
-
-            @pl.when(i == T - 1)
+
+                @pl.when(g <= 1)
+                def _():
+                    zsend(g, j).start()
+
+            @pl.when(i == 0)
             def _():
                 X[z, y, c, j] = blk
                 ysend(0, j).start()
@@ -176,21 +179,27 @@
 
     lax.fori_loop(0, T, pack, 0)
 
+    wt[0] = pw[0].astype(F32).T.astype(BF)
+    wt[1] = pw[1].astype(F32).T.astype(BF)
     n0, n1 = HI, R - LO
     m0 = lax.broadcasted_iota(jnp.int32, (2, n0, HS), 1).reshape(2 * n0, HS) < 2 * CAP
     m1 = lax.broadcasted_iota(jnp.int32, (2, n1, HS), 1).reshape(2 * n1, HS) >= 2 * CAP - LO
 
-    def hidden_of(s, a):
-        lo, n, m = ((0, n0, m0), (LO, n1, m1))[a]
-        acc = None
-        for h in range(2):
-            for j in range(NC):
-                x = X[s, :, h, j, lo:lo + n, :].reshape(2 * n, HC)
-                v = dot(x, wg[a, h * H + j * HC:h * H + (j + 1) * HC, :])
-                acc = v if acc is None else acc + v
+    spans = ((0, n0, m0), (LO, n1, m1))
+
+    def up_part(s, hh, j, acc):
+        at = pl.ds(pl.multiple_of(hh * H + j * HC, 128), HC)
+        new = []
+        for a, (lo, n, m) in enumerate(spans):
+            x = X[s, :, hh, j, lo:lo + n, :].reshape(2 * n, HC)
+            v = dot(x, wg[a, at, :])
+            new.append(v if acc is None else acc[a] + v)
+        return new
+
+    def act(a, acc):
         gt, up = acc[:, :HS], acc[:, HS:]
         hid = gt / (1.0 + jnp.exp(-gt)) * up
-        return jnp.where(m, hid, 0.0).astype(BF)
+        return jnp.where(spans[a][2], hid, 0.0).astype(BF)
 
     def down(h0, h1, hh, j, store):
         o0 = dot(h0, wd[0, hh, j]).reshape(2, n0, HC)
@@ -210,6 +219,10 @@
                 ysend(k, j).start()
                 csend_a(k, j).start()
 
+                @pl.when(k + 1 < T)
+                def _():
+                    zsend(k + 1, j).start()
+
         @pl.when((k >= 1) & (k < T + 1))
         def _():
             g = k - 1
@@ -223,11 +236,15 @@
                 for w in wcopies:
                     w.wait()
 
+            acc = None
+            for j in range(NC):
+                acc = up_part(s, c, j, acc)
             for j in range(NC):
                 xcopy(2, s, y, 1 - c, g, j, e_core).wait_recv()
                 xcopy(3, s, 1 - y, 1 - c, g, j, e_core).wait_recv()
-            h0 = hidden_of(s, 0)
-            h1 = hidden_of(s, 1)
+                acc = up_part(s, 1 - c, j, acc)
+            h0 = act(0, acc[0])
+            h1 = act(1, acc[1])
             for j in range(NC):
                 def put(lo, hi, v, j=j):
                     ps[g, j, :, lo:hi, :] = v.astype(BF)
@@ -269,8 +286,6 @@
 
     lax.fori_loop(0, T + 2, step, 0)
 
-    w1 = pw[0].astype(F32).T.astype(BF)
-    w2 = pw[1].astype(F32).T.astype(BF)
     orow = pl.ds(pl.multiple_of((1 - c) * TOK, 16), TOK)
     fl = []
     fc = []
@@ -283,7 +298,7 @@
 
         lax.fori_loop(1, T, got, 0)
         back = ret[j].reshape(TR, HC)
-        fin[j] = (dot(w1, back) + dot(w2, back)).astype(BF)
+        fin[j] = (dot(wt[0], back) + dot(wt[1], back)).astype(BF)
 
         def cols(i, j=j):
             return pl.ds(pl.multiple_of(i * H + j * HC, 128), HC)
@@ -338,7 +353,7 @@
             functools.partial(kernel, T, cap, R, lo, hi, NC),
             out_shape=jax.ShapeDtypeStruct((tok, d), BF),
             in_specs=[anym, anym, anym, anym, anym, vm, vm, pl.BlockSpec(memory_space=pltpu.SMEM)],
-            out_specs=vm,
+            out_specs=anym,
             scratch_shapes=[
                 pltpu.VMEM((2, d, 2 * hs), BF),
                 pltpu.VMEM((2, 2, NC, hs, hc), BF),
@@ -356,6 +371,7 @@
                 pltpu.VMEM((T, NC, R, hc), BF),
                 pltpu.VMEM((NC, T, R, hc), BF),
                 pltpu.VMEM((NC, 2 * tok, hc), BF),
+                pltpu.VMEM((2, 2 * tok, T * R), BF),
                 pltpu.SemaphoreType.DMA((1 + NC,)),
                 pltpu.SemaphoreType.DMA((3, 2 * NC)),
                 pltpu.SemaphoreType.DMA((7, T, NC)),

time: 76.7 us -> 73.6 us (0.960); the launches traced: 75.3 us -> 73 us
  Pallas kernels: 72.8 us -> 70.5 us
    pallas_call x1, Pallas kernels: 72.8 us -> 70.5 us  [local(): pl.pallas_call(functools.partial(kernel, T, cap, R, lo, hi, NC), out_shap...]
where the time goes in v3:
time: 73.6 us; the launch traced here: 73 us
  Pallas kernels  70.5 us (96%)
  local copies, waits for them, and re-layouts  1.82 us (2%)
    pallas_call x1, Pallas kernels, local(): pl.pallas_call(functools.partial(kernel, T, cap, R, lo, hi, NC), out_shap...  70.5 us
    unnamed x1, local copies, waits for them, and re-layouts  1.82 us

profile of v3, /device:TPU:9, one launch (start us, length us, event | category | flops | bytes accessed | tf_op | source)
XLA Modules:
  0.0 73.0 jit_solution(18047257697538844208)
XLA Ops:
  0.7 70.5 %shard_map.82 = bf16[64,3584]{1,0:T(8,128)(2,1)} custom-call(bf16[64,3584]{1,0:T(8,128)(2,1)} %tok_ref.1, bf16[1,3584,512]{2,1,0:T(8,128)(2,1)} %wg_ref.1, bf16[1,256,3584]{2,1,0:T(8,128)(2,1)} %wd_ref.1, bf16[1,3584,512]{2,1,0:T(8,128)(2,1)} %cg_ref.1, bf16[1,256,3584]{2,1,0:T(8,128)(2,1)} %cd_ref.1, s32[2,64]{1,0:T(2,128)} %bitcast.2, f32[2,64]{1,0:T(2,128)} %bitcast.3, ...), custom_call_target="tpu_custom_call" | custom-call | tf_op jit(solution)/shard_map/pallas_call | solution.py:352
  71.2 1.8 %copy.11 = bf16[64,3584]{1,0:T(8,128)(2,1)} copy(bf16[64,3584]{1,0:T(8,128)(2,1)} %shard_map.82) | data formatting | bytes 917504

commit v4 on v3

--- a/solution.py
+++ b/solution.py
@@ -216,12 +216,13 @@
         def _():
             for j in range(NC):
                 zrecv(k, j).wait_recv()
-                ysend(k, j).start()
-                csend_a(k, j).start()
 
                 @pl.when(k + 1 < T)
                 def _():
                     zsend(k + 1, j).start()
+
+                ysend(k, j).start()
+                csend_a(k, j).start()
 
         @pl.when((k >= 1) & (k < T + 1))
         def _():

time: 73.6 us -> 73.6 us (level)
  no operation moved by 1% of the time
where the time goes in v4:
time: 73.6 us; the launch traced here: 73 us
  Pallas kernels  70.5 us (96%)
  local copies, waits for them, and re-layouts  1.82 us (2%)
    pallas_call x1, Pallas kernels, local(): pl.pallas_call(functools.partial(kernel, T, cap, R, lo, hi, NC), out_shap...  70.5 us
    unnamed x1, local copies, waits for them, and re-layouts  1.82 us

profile of v4, /device:TPU:9, one launch (start us, length us, event | category | flops | bytes accessed | tf_op | source)
XLA Modules:
  0.0 73.0 jit_solution(11868081410284690518)
XLA Ops:
  0.7 70.5 %shard_map.82 = bf16[64,3584]{1,0:T(8,128)(2,1)} custom-call(bf16[64,3584]{1,0:T(8,128)(2,1)} %tok_ref.1, bf16[1,3584,512]{2,1,0:T(8,128)(2,1)} %wg_ref.1, bf16[1,256,3584]{2,1,0:T(8,128)(2,1)} %wd_ref.1, bf16[1,3584,512]{2,1,0:T(8,128)(2,1)} %cg_ref.1, bf16[1,256,3584]{2,1,0:T(8,128)(2,1)} %cd_ref.1, s32[2,64]{1,0:T(2,128)} %bitcast.2, f32[2,64]{1,0:T(2,128)} %bitcast.3, ...), custom_call_target="tpu_custom_call" | custom-call | tf_op jit(solution)/shard_map/pallas_call | solution.py:353
  71.2 1.8 %copy.11 = bf16[64,3584]{1,0:T(8,128)(2,1)} copy(bf16[64,3584]{1,0:T(8,128)(2,1)} %shard_map.82) | data formatting | bytes 917504
